TPU v7x, 512 devices: a whole 4x4x16 slice. The times are simulated.
512 devices in a mesh: dp: 32 (over z, x_hi), tensor: 16 (over x_lo, y, core).
Axes of the slice: x: 4 (x_hi: 2, x_lo: 2; x = x_hi * 2 + x_lo), y: 4, z: 16, core: 2. Of those that a mesh axis runs over, the one named last changes fastest.
Arguments:
- acts: bfloat16 [32768, 28672], P('dp', 'tensor'), may hold values from -6 to 6
Outputs:
- factor_tiles: float32 [896, 16, 2, 896], P('dp', 'tensor')
All inputs are finite; a program needn't handle non-finite values.
Results may differ from a plain program's by a relative error of at most 0.0003.
Values may be sent and summed in bfloat16 or wider, within the bound.
A program may use at most 64 MiB of HBM per device.

v0:
```python
import jax
import jax.numpy as jnp
from jax import lax
from jax.sharding import PartitionSpec as P

FROWS = 896
COLS = 896


def passed_along(block, axis, distance):
    devices = range(lax.axis_size(axis))
    route = [((i - distance) % len(devices), i) for i in devices]
    return lax.ppermute(block, axis, route)


def tile_rows(window, other, scale):
    product = lax.dot_general(
        window, other, (((0,), (0,)), ((), ())), preferred_element_type=jnp.float32
    )
    return product * scale


def per_device(acts):
    scale = 1.0 / (acts.shape[0] * lax.axis_size("dp"))
    window = acts[:, :FROWS]
    columns = acts[:, :COLS]
    pairs = [(window, columns), (window, passed_along(columns, "tensor", 1))]
    stacked = jnp.stack([tile_rows(left, right, scale) for left, right in pairs], axis=1)
    shares = lax.all_to_all(stacked[None], "dp", split_axis=1, concat_axis=0, tiled=True)
    summed = jnp.sum(shares, axis=0)[:, None, :, :]
    first_tile = summed[:, :, 0:1, :]
    second_tile = summed[:, :, 1:2, :]
    return jnp.concatenate([first_tile, second_tile], axis=2)


def solution(mesh):
    return jax.shard_map(
        per_device,
        mesh=mesh,
        in_specs=(P("dp", "tensor"),),
        out_specs=P("dp", "tensor", None, None),
        check_vma=False,
    )
```

profile of v0, /device:TPU:24, one launch (start us, length us, event | category | flops | bytes accessed | tf_op | source)
XLA Modules:
  0.0 351.0 jit_solution(1124620277269135597)
XLA Ops:
  0.0 0.0 copy-start
  0.0 1.8 slice.3
  1.8 1.9 collective-permute-start
  3.7 0.0 copy-done
  3.7 2.1 multiply_bitcast_fusion.1
  5.9 20.5 %collective-permute-done = bf16[1024,896]{1,0:T(8,128)(2,1)S(1)} collective-permute-done((bf16[1024,896]{1,0:T(8,128)(2,1)S(1)}, bf16[1024,896]{1,0:T(8,128)(2,1)S(1)}, u32[]{:S(2)}, u32[]{:S(2)}) %collective-permute-start) | collective-permute-done | bytes 1835040 | tf_op jit(solution)/shard_map/ppermute | solution.py:13
  26.3 2.1 multiply_bitcast_fusion
  28.5 3.1 maximum_bitcast_fusion
  31.6 10.5 %copy.3 = f32[1,896,2,896]{3,2,0,1:T(2,128)} copy(f32[1,896,2,896]{3,1,2,0:T(8,128)} %maximum_bitcast_fusion) | data formatting | bytes 12845056 | tf_op jit(solution)/shard_map/broadcast_in_dim | solution.py:29
  42.1 303.6 %all_to_all.12 = f32[1,896,2,896]{3,2,0,1:T(2,128)} all-to-all(f32[1,896,2,896]{3,2,0,1:T(2,128)} %copy.3), channel_id=1, replica_groups=mesh['dp'=32,'tensor'=16] {'dp'}, dimensions={1} | all-to-all | bytes 12845056 | tf_op jit(solution)/shard_map/all_to_all | solution.py:29
  345.7 5.3 %reduce_sum.9 = f32[28,2,896]{2,1,0:T(2,128)} reduce(f32[32,28,2,896]{3,2,1,0:T(2,128)} %bitcast.9, f32[]{:T(128)} %constant.1.clone.1), dimensions={0}, to_apply=%region_0.0 | reduce | flops 1555456 | bytes 6623236 | tf_op jit(solution)/shard_map/reduce_sum | solution.py:30
Async XLA Ops:
  0.0 3.7 %copy-start = (bf16[1024,1792]{1,0:T(8,128)(2,1)S(1)}, bf16[1024,1792]{1,0:T(8,128)(2,1)}, u32[]{:S(2)}) copy-start(bf16[1024,1792]{1,0:T(8,128)(2,1)} %param.1) | copy-start | bytes 11010052
  1.8 24.5 %collective-permute-start = (bf16[1024,896]{1,0:T(8,128)(2,1)S(1)}, bf16[1024,896]{1,0:T(8,128)(2,1)S(1)}, u32[]{:S(2)}, u32[]{:S(2)}) collective-permute-start(bf16[1024,896]{1,0:T(8,128)(2,1)S(1)} %slice.3), channel_id=1, source_target_pairs={{15,0},{0,1},{1,2},{2,3},{3,4},{4,5},{5,6},{6,7},{7,8},{8,9},{9,10... | collective-permute-start | bytes 5505032 | tf_op jit(solution)/shard_map/ppermute | solution.py:13
where the time goes:
time: 352 us; the launch traced here: 351 us
  blocking collectives  304 us (86%)
  waiting for transfers between devices  20.5 us (6%)
  local copies, waits for them, and re-layouts  12.3 us (3%)
  other arithmetic  8.42 us (2%)
  matrix products  4.26 us (1%)
    all_to_all x1, blocking collectives, per_device(): lax.all_to_all(stacked[None], 'dp', split_axis=1, concat_axis=0, tiled=True)  304 us
    ppermute x1, waiting for transfers between devices, passed_along(): return lax.ppermute(block, axis, route)  20.5 us
    broadcast_in_dim x1, local copies, waits for them, and re-layouts, per_device(): stacked[None]  10.5 us
  transfers between devices with their start and end apart: 1, of which 1 were waited for; matrix products, arithmetic and copies ran while one was open for 1% of the time, Pallas kernels for 0%

commit v1 on v0

v1 whole, which is shorter than its diff:
```python
import jax
import jax.numpy as jnp
from jax import lax
from jax.experimental import pallas as pl
from jax.experimental.pallas import tpu as pltpu
from jax.sharding import PartitionSpec as P

ROWS = 896
COLS = 896
LANES = 128
MESH = pl.DeviceIdType.MESH
TN = (((0,), (0,)), ((), ()))

POWER = 17
TOP = 2.0**7.375

STREAMS = ((0, 0, 4), (0, 4, 3), (1, 0, 4), (1, 4, 3))
LAGS = ((0, 0, 1, 2), (0, 0, 2, 4))
SCALE_ROWS = 16


def round_up(n, m):
    return (n + m - 1) // m * m


def encode(value, factor):
    u = value * factor
    u2 = u * u
    u4 = u2 * u2
    u8 = u4 * u4
    return u8 * u8 * u


def decode(code, factor):
    y = code.astype(jnp.float32)
    size = jnp.exp2(jnp.log2(jnp.abs(y)) * (1.0 / POWER)) * factor
    return jnp.where(y == 0.0, 0.0, jnp.where(y < 0.0, -size, size))


def groups(blocks):
    out = [(2 * i, 2) for i in range(blocks // 2)]
    if blocks % 2:
        out.append((blocks - 1, 1))
    return out


def lane_max(values):
    n = values.shape[0] // 8
    return jnp.max(jnp.abs(values).reshape(n, 8, LANES), axis=0)


def scale_of(top):
    top = jnp.max(top, axis=0, keepdims=True)
    return (top * 1.008 + 1e-36).astype(jnp.bfloat16).astype(jnp.float32)


def kernel(nz, acts_ref, out_ref, mine, other, part0, part1, held, *rest):
    ns = len(STREAMS)
    got = rest[:ns]
    put = rest[ns : 2 * ns]
    xgot = rest[2 * ns : 3 * ns]
    xput = rest[3 * ns : 4 * ns]
    kept = rest[4 * ns : 5 * ns]
    load_sem, wsend, wrecv, rsend, rrecv, xsend, xrecv = rest[5 * ns :]
    parts = (part0, part1)
    chunk = ROWS // nz
    half = chunk // 2
    wide = round_up(half, 8)

    dp = lax.axis_index("dp")
    t = lax.axis_index("tensor")
    ndp = 2 * nz
    nt = lax.axis_size("tensor")
    z, xh = dp // 2, lax.rem(dp, 2)
    core = lax.rem(t, 2)
    ahead = (lax.rem(dp + 2, ndp), t)
    behind = (lax.rem(dp + ndp - 2, ndp), t)
    across = (dp + 1 - 2 * xh, t)
    right = (dp, lax.rem(t + 1, nt))
    left = (dp, lax.rem(t + nt - 1, nt))

    load = pltpu.make_async_copy(acts_ref.at[:, 0:COLS], mine, load_sem)
    load.start()
    barrier = pltpu.get_barrier_semaphore()
    for device in (ahead, behind, across, right, left):
        pl.semaphore_signal(barrier, inc=1, device_id=device, device_id_type=MESH)
    load.wait()
    pl.semaphore_wait(barrier, 5)

    windows = []
    for i, (a, b) in enumerate(((0, 512), (512, 896))):
        windows.append(
            pltpu.make_async_remote_copy(
                src_ref=mine.at[:, a:b],
                dst_ref=other.at[:, a:b],
                send_sem=wsend.at[i],
                recv_sem=wrecv.at[i],
                device_id=right,
                device_id_type=MESH,
            )
        )
    for copy in windows:
        copy.start()

    part0[...] = lax.dot_general(mine[...], mine[...], TN, preferred_element_type=jnp.float32)

    def hops(i, d):
        return nz // 2 - (d + i) % 2

    def message(i, d, k):
        return pltpu.make_async_remote_copy(
            src_ref=put[i].at[d, k],
            dst_ref=got[i].at[d, k],
            send_sem=rsend.at[i, d, k],
            recv_sem=rrecv.at[i, d, k],
            device_id=behind if d else ahead,
            device_id_type=MESH,
        )

    def swap(i):
        return pltpu.make_async_remote_copy(
            src_ref=xput[i],
            dst_ref=xgot[i],
            send_sem=xsend.at[i],
            recv_sem=xrecv.at[i],
            device_id=across,
            device_id_type=MESH,
        )

    def partial(i, g, n, owner):
        tile, first, _ = STREAMS[i]
        rows = pl.ds(pl.multiple_of(owner * chunk, 8), chunk)
        pieces = [
            parts[tile][rows, (first + g + j) * LANES : (first + g + j + 1) * LANES]
            for j in range(n)
        ]
        return jnp.concatenate(pieces, axis=0) if n > 1 else pieces[0]

    def factor_in(ref, at):
        return ref[at : at + SCALE_ROWS, :].astype(jnp.float32)[0:1] * (1.0 / TOP)

    def unpack(ref, a, n, factor):
        size = round_up(n, 16)
        return decode(ref[a : a + size, :], factor)[:n]

    def pack(src, ref, spans, top, tail):
        scale = scale_of(top)
        factor = TOP / scale
        for a, n in spans:
            ref[a : a + n, :] = encode(src[a : a + n, :], factor).astype(jnp.bfloat16)
        ref[tail : tail + SCALE_ROWS, :] = jnp.broadcast_to(scale, (SCALE_ROWS, LANES)).astype(
            jnp.bfloat16
        )

    def step(i, d, k):
        blocks = STREAMS[i][2]
        length = hops(i, d)
        sign = -1 if d else 1
        owner = lax.rem(z + sign * (length - k) + 2 * nz, nz)
        body = round_up(blocks * chunk, 16)

        @pl.when(k == 0)
        def _():
            for g, n in groups(blocks):
                held[g * chunk : (g + n) * chunk, :] = partial(i, g, n, owner)

        @pl.when(k > 0)
        def _():
            message(i, d, k - 1).wait_recv()
            ref = got[i].at[d, k - 1]
            factor = factor_in(ref, body)
            for g, n in groups(blocks):
                held[g * chunk : (g + n) * chunk, :] = partial(i, g, n, owner) + unpack(
                    ref, g * chunk, n * chunk, factor
                )

        top = jnp.zeros((8, LANES), jnp.float32)
        for g, n in groups(blocks):
            top = jnp.maximum(top, lane_max(held[g * chunk : (g + n) * chunk, :]))
        spans = [(g * chunk, round_up(n * chunk, 16)) for g, n in groups(blocks)]
        pack(held, put[i].at[d, k], spans, top, body)
        message(i, d, k).start()

    def finish(i):
        blocks = STREAMS[i][2]
        body = round_up(blocks * chunk, 16)
        refs = []
        for d in range(2):
            last = hops(i, d) - 1
            message(i, d, last).wait_recv()
            refs.append(got[i].at[d, last])
        factors = [factor_in(ref, body) for ref in refs]
        top = jnp.zeros((8, LANES), jnp.float32)
        for g, n in groups(blocks):
            total = partial(i, g, n, z)
            for ref, factor in zip(refs, factors):
                total = total + unpack(ref, g * chunk, n * chunk, factor)
            for j in range(n):
                low = total[j * chunk : j * chunk + wide]
                high = total[(j + 1) * chunk - wide : (j + 1) * chunk]
                at = (g + j) * wide
                kept[i][at : at + wide, :] = jnp.where(xh == 0, low, high)
                away = jnp.where(xh == 0, high, low)
                held[at : at + wide, :] = away
                top = jnp.maximum(top, lane_max(away))
        spans = [(j * wide, wide) for j in range(blocks)]
        pack(held, xput[i], spans, top, blocks * wide)
        swap(i).start()

    def deliver(i):
        tile, first, blocks = STREAMS[i]
        swap(i).wait_recv()
        factor = factor_in(xgot[i], blocks * wide)
        inverse = 1.0 / (1024 * ndp)
        for j in range(blocks):
            at = j * wide
            total = (kept[i][at : at + wide, :] + unpack(xgot[i], at, wide, factor)) * inverse
            value = jnp.where(xh == 0, total[:half], total[wide - half :])
            out_ref[pl.ds(2 * (first + j) + tile, half, stride=2 * (COLS // LANES)), :] = value

    def lag(i):
        return jnp.where(core == 0, LAGS[1][i], LAGS[0][i])

    last = nz // 2

    def tick(now, _):
        for i, (tile, first, blocks) in enumerate(STREAMS):
            k = now - lag(i)
            if tile:
                a, b = first * LANES, (first + blocks) * LANES

                @pl.when(k == 0)
                def _():
                    windows[i - 2].wait_recv()
                    part1[:, a:b] = lax.dot_general(
                        mine[...], other[:, a:b], TN, preferred_element_type=jnp.float32
                    )

            for d in range(2):

                @pl.when((k >= 0) & (k < hops(i, d)))
                def _():
                    step(i, d, k)

            @pl.when(k == last)
            def _():
                finish(i)

            @pl.when(k == last + 1)
            def _():
                deliver(i)

        return 0

    lax.fori_loop(0, max(map(max, LAGS)) + last + 2, tick, 0)

    for copy in windows:
        copy.wait_send()
    for i in range(ns):
        for d in range(2):
            for k in range(hops(i, d)):
                message(i, d, k).wait_send()
        swap(i).wait_send()


def per_device(acts):
    nz = lax.axis_size("dp") // 2
    chunk = ROWS // nz
    half = chunk // 2
    wide = round_up(half, 8)
    depth = nz // 2
    ns = len(STREAMS)
    body = [round_up(b * chunk, 16) + SCALE_ROWS for _, _, b in STREAMS]
    xbody = [b * wide + SCALE_ROWS for _, _, b in STREAMS]
    scratch = [
        pltpu.VMEM((acts.shape[0], COLS), jnp.bfloat16),
        pltpu.VMEM((acts.shape[0], COLS), jnp.bfloat16),
        pltpu.VMEM((ROWS, COLS), jnp.float32),
        pltpu.VMEM((ROWS, COLS), jnp.float32),
        pltpu.VMEM((max(body), LANES), jnp.float32),
    ]
    scratch += [pltpu.VMEM((2, depth, n, LANES), jnp.bfloat16) for n in body] * 2
    scratch += [pltpu.VMEM((n, LANES), jnp.bfloat16) for n in xbody] * 2
    scratch += [pltpu.VMEM((n - SCALE_ROWS, LANES), jnp.float32) for n in xbody]
    dma = pltpu.SemaphoreType.DMA
    scratch += [dma, dma((2,)), dma((2,)), dma((ns, 2, depth)), dma((ns, 2, depth)), dma((ns,)), dma((ns,))]
    flat = pl.pallas_call(
        lambda *refs: kernel(nz, *refs),
        out_shape=jax.ShapeDtypeStruct((half * 2 * (COLS // LANES), LANES), jnp.float32),
        in_specs=[pl.BlockSpec(memory_space=pl.ANY)],
        out_specs=pl.BlockSpec(memory_space=pltpu.VMEM),
        scratch_shapes=scratch,
        compiler_params=pltpu.CompilerParams(
            collective_id=0, has_side_effects=True, vmem_limit_bytes=48 * 2**20
        ),
        cost_estimate=pl.CostEstimate(
            flops=4 * ROWS * COLS * acts.shape[0], bytes_accessed=2 * acts.size, transcendentals=0
        ),
    )(acts)
    tiles = flat.reshape(half, COLS // LANES, 2, LANES).transpose(0, 2, 1, 3)
    return tiles.reshape(half, 1, 2, COLS)


def solution(mesh):
    return jax.shard_map(
        per_device,
        mesh=mesh,
        in_specs=(P("dp", "tensor"),),
        out_specs=P("dp", "tensor", None, None),
        check_vma=False,
    )
```

time: 352 us -> 74.5 us (0.21)
  the two profiles are of different devices: /device:TPU:24 before, /device:TPU:2 now
where the time goes in v1:
time: 74.5 us; the launch traced here: 74.4 us
  Pallas kernels  71.5 us (96%)
  local copies, waits for them, and re-layouts  2.86 us (4%)
    pallas_call x1, Pallas kernels, per_device(): pl.pallas_call(lambda *refs: kernel(nz, *refs), out_shape=jax.ShapeDtypeS...  71.5 us
    unnamed x2, local copies, waits for them, and re-layouts  2.04 us

profile of v1, /device:TPU:2, one launch (start us, length us, event | category | flops | bytes accessed | tf_op | source)
XLA Modules:
  0.0 74.4 jit_solution(16809544107989123536)
XLA Ops:
  0.0 0.0 copy-start
  0.0 2.0 %copy-done = bf16[1024,1792]{1,0:T(8,128)(2,1)S(1)} copy-done((bf16[1024,1792]{1,0:T(8,128)(2,1)S(1)}, bf16[1024,1792]{1,0:T(8,128)(2,1)}, u32[]{:S(2)}) %copy-start) | copy-done | bytes 3670040
  2.0 71.5 %shard_map.17 = f32[392,128]{1,0:T(8,128)S(1)} custom-call(bf16[1024,1792]{1,0:T(8,128)(2,1)S(1)} %copy-done), custom_call_target="tpu_custom_call" | custom-call | flops 3288334336 | bytes 3670016 | tf_op jit(solution)/shard_map/pallas_call | solution.py:287
  73.6 0.8 %reshape.7 = f32[28,1,2,896]{3,2,0,1:T(2,128)} reshape(f32[28,2,7,128]{3,2,1,0:T(8,128)S(1)} %bitcast.6) | data formatting | bytes 401408 | tf_op jit(solution)/shard_map/reshape | solution.py:301
  (1 shorter events, 0.0 us)
Async XLA Ops:
  0.0 2.0 %copy-start = (bf16[1024,1792]{1,0:T(8,128)(2,1)S(1)}, bf16[1024,1792]{1,0:T(8,128)(2,1)}, u32[]{:S(2)}) copy-start(bf16[1024,1792]{1,0:T(8,128)(2,1)} %refs_0_.1) | copy-start | bytes 11010052

commit v2 on v0

v2 whole, which is shorter than its diff:
```python
import jax
import jax.numpy as jnp
from jax import lax
from jax.experimental import pallas as pl
from jax.experimental.pallas import tpu as pltpu
from jax.sharding import PartitionSpec as P

ROWS = 896
COLS = 896
LANES = 128
BLOCKS = COLS // LANES
MESH = pl.DeviceIdType.MESH
TN = (((0,), (0,)), ((), ()))

POWER = 17
TOP = 2.0**7.375

STREAMS = ((0, 0, 4), (0, 4, 3), (1, 0, 4), (1, 4, 3))
STARTS = ((0, 0, 0, 0), (0, 0, 2, 5))
CHAINS = ((8, 8, 8, 8), (8, 8, 8, 4))
PIECES = 2
JUMPS = (1, 5)
TICKS = 12


def by_core(core, table):
    return jnp.where(core == 0, table[0], table[1])


def scaled(value, factor):
    return (value.reshape(value.shape[0] // 8, 8, LANES) * factor).reshape(value.shape)


def encode(value, factor):
    u = scaled(value, factor)
    u2 = u * u
    u4 = u2 * u2
    u8 = u4 * u4
    return u8 * u8 * u


def decode(code, factor):
    y = code.astype(jnp.float32)
    size = scaled(jnp.exp2(jnp.log2(jnp.abs(y)) * (1.0 / POWER)), factor)
    return jnp.where(y < 0.0, -size, size)


def tops(values):
    out = None
    for value in values:
        top = jnp.max(jnp.abs(value).reshape(value.shape[0] // 8, 8, LANES), axis=0)
        out = top if out is None else jnp.maximum(out, top)
    return out


class Packet:
    def __init__(self, sizes):
        self.spans = []
        at = 0
        for n in sizes:
            self.spans.append((at, n))
            at += n
        self.body = at
        self.rows = (at // 16 + 1) * 16
        self.tail = self.rows - at

    def read(self, ref):
        bound = ref[self.rows - 16 : self.rows, :].astype(jnp.float32)[8:]
        factor = bound * (1.0 / TOP)
        values = [decode(ref[at : at + (n + 15) // 16 * 16, :], factor)[:n] for at, n in self.spans]
        return values, bound

    def write(self, values, ref, bound):
        bound = (bound * 1.008 + 1e-36).astype(jnp.bfloat16).astype(jnp.float32)
        factor = TOP / bound
        rest = jnp.concatenate([bound] * (self.tail // 8), axis=0)
        for value, (at, n) in zip(values, self.spans):
            code = encode(value, factor)
            if n % 16:
                code = jnp.concatenate([code, rest], axis=0)
            ref[at : at + code.shape[0], :] = code.astype(jnp.bfloat16)
        if self.body % 16 == 0:
            ref[self.body : self.rows, :] = rest.astype(jnp.bfloat16)


def add(some, more):
    return [x + y for x, y in zip(some, more)]


PACKETS = tuple(Packet((112,) * (n // 2) + (56,) * (n % 2)) for _, _, n in STREAMS)
SWAPS = tuple(Packet((32,) * n) for _, _, n in STREAMS)


def kernel(nz, acts_ref, out_ref, mine, pair, other, part0, part1, peaks, *rest):
    ns = len(STREAMS)
    got, put, late_got, late_put = (rest[k * ns : (k + 1) * ns] for k in range(4))
    kept, load_sem, psend, precv, wsend, wrecv, rsend, rrecv, lsend, lrecv = rest[4 * ns :]
    parts = (part0, part1)
    chunk = ROWS // nz
    depth = nz // 2

    dp = lax.axis_index("dp")
    t = lax.axis_index("tensor")
    ndp = 2 * nz
    nt = lax.axis_size("tensor")
    z, xh = lax.div(dp, 2), lax.rem(dp, 2)
    core = lax.rem(t, 2)
    even = xh == 0

    def along(hops):
        return (lax.rem(dp + 2 * hops + 2 * ndp, ndp), t)

    twin = dp + 1 - 2 * xh
    across = (twin, t)
    mate = t + 1 - 2 * core
    right, left = lax.rem(t + 2, nt), lax.rem(t + nt - 2, nt)

    load = pltpu.make_async_copy(acts_ref.at[:, 0:COLS], mine, load_sem)
    load.start()
    barrier = pltpu.get_barrier_semaphore()
    partners = [along(sign * jump) for jump in JUMPS for sign in (1, -1)]
    partners += [across, (dp, mate), (twin, mate), (dp, right), (dp, left)]
    for device in partners:
        pl.semaphore_signal(barrier, inc=1, device_id=device, device_id_type=MESH)
    load.wait()
    for i in range(ns):
        for d in range(2):
            got[i][d, depth] = jnp.zeros(got[i].shape[2:], jnp.bfloat16)

    def own_rows(i, owner):
        tile, first, _ = STREAMS[i]
        rows = pl.ds(pl.multiple_of(owner * chunk, 8), chunk)
        values = []
        for at, n in PACKETS[i].spans:
            j = first + at // chunk
            pieces = [
                parts[tile][rows, (j + m) * LANES : (j + m + 1) * LANES] for m in range(n // chunk)
            ]
            values.append(jnp.concatenate(pieces, axis=0) if len(pieces) > 1 else pieces[0])
        return values

    second = [tile for tile, _, _ in STREAMS].index(1)

    def columns(i):
        _, first, blocks = STREAMS[i]
        return first * LANES, (first + blocks) * LANES

    def multiply(i, left_ref, right_ref):
        a, b = columns(i)
        parts[STREAMS[i][0]][:, a:b] = lax.dot_general(
            left_ref[...], right_ref[:, a:b], TN, preferred_element_type=jnp.float32
        )

    def measure(i):
        def peak(owner, _):
            peaks[i, owner] = tops(own_rows(i, owner))
            return 0

        lax.fori_loop(0, nz, peak, 0)

    for i in range(second):
        multiply(i, mine, mine)
        measure(i)
    pl.semaphore_wait(barrier, len(partners))

    exchange = pltpu.make_async_remote_copy(
        src_ref=mine,
        dst_ref=pair,
        send_sem=psend,
        recv_sem=precv,
        device_id=(dp, mate),
        device_id_type=MESH,
    )
    exchange.start()

    def window(i):
        a, b = columns(i)
        return pltpu.make_async_remote_copy(
            src_ref=mine.at[:, a:b],
            dst_ref=other.at[:, a:b],
            send_sem=wsend.at[i],
            recv_sem=wrecv.at[i],
            device_id=(dp, right),
            device_id_type=MESH,
        )

    @pl.when(core == 1)
    def _():
        for i in range(second, ns):
            window(i).start()

    def reach(i, d):
        return depth - lax.rem(d + i, 2)

    def chain(i):
        return by_core(core, [c[i] for c in CHAINS])

    def message(i, d, hop, target):
        return pltpu.make_async_remote_copy(
            src_ref=put[i].at[d, hop - 1],
            dst_ref=got[i].at[d, hop - 1],
            send_sem=rsend.at[i, d, hop - 1],
            recv_sem=rrecv.at[i, d, hop - 1],
            device_id=target,
            device_id_type=MESH,
        )

    def late(i, which):
        target = (twin if which else dp, mate if STREAMS[i][0] else t)
        return pltpu.make_async_remote_copy(
            src_ref=late_put[i].at[which],
            dst_ref=late_got[i].at[which],
            send_sem=lsend.at[i, which],
            recv_sem=lrecv.at[i, which],
            device_id=target,
            device_id_type=MESH,
        )

    def step(i, d, hop, length):
        sign = 1 - 2 * d
        owner = lax.rem(z + sign * hop + nz, nz)
        outermost = (hop == reach(i, d)) | (lax.rem(hop, length) == 0)

        @pl.when(jnp.logical_not(outermost))
        def _():
            message(i, d, hop + 1, across).wait_recv()

        values, bound = own_rows(i, owner), peaks[i, owner]
        more, more_bound = PACKETS[i].read(got[i].at[d, jnp.where(outermost, depth, hop)])
        PACKETS[i].write(add(values, more), put[i].at[d, hop - 1], bound + more_bound)
        jump = jnp.where(lax.rem(hop, length) == 1, hop, 1)
        message(i, d, hop, along(sign * jump)).start()

    def tick_of(i, k):
        length = chain(i)

        def one(j, _):
            d, m = lax.rem(j, 2), lax.div(j, 2)
            hop = (m + 1) * length - k

            @pl.when((k >= 0) & (k < length) & (hop <= reach(i, d)))
            def _():
                step(i, d, hop, length)

            return 0

        lax.fori_loop(0, 2 * PIECES, one, 0)

    def gather(i):
        length = chain(i)
        values, bound = own_rows(i, z), peaks[i, z]
        for m in range(PIECES):
            for d in range(2):
                hop = m * length + 1
                here = hop <= reach(i, d)

                @pl.when(here)
                def _():
                    message(i, d, hop, across).wait_recv()

                more, more_bound = PACKETS[i].read(got[i].at[d, jnp.where(here, hop - 1, depth)])
                values, bound = add(values, more), bound + more_bound
        return values, bound

    inverse = 1.0 / (1024 * ndp)
    stride = 2 * BLOCKS

    def finish(i):
        tile, _, blocks = STREAMS[i]
        values, bound = gather(i)
        total = jnp.concatenate(values, axis=0)
        here, away = [], []
        for block in range(blocks):
            low = total[block * chunk : block * chunk + 32]
            high = total[(block + 1) * chunk - 32 : (block + 1) * chunk]
            here.append(jnp.where(even, low, high))
            away.append(jnp.where(even, high, low))
        SWAPS[i].write(away, late_put[i].at[1], bound)
        late(i, 1).start()
        if tile:
            SWAPS[i].write(here, late_put[i].at[0], bound)
            late(i, 0).start()
        else:
            for block in range(blocks):
                at = 32 * (STREAMS[i][1] + block)
                kept[at : at + 32, :] = here[block]

    def deliver(i):
        tile, first, blocks = STREAMS[i]
        late(i, 1).wait_recv()
        values, _ = SWAPS[i].read(late_got[i].at[1])
        if tile:
            late(i, 0).wait_recv()
            others, _ = SWAPS[i].read(late_got[i].at[0])
        else:
            others = [kept[32 * j : 32 * j + 32, :] for j in range(first, first + blocks)]
        for block in range(blocks):
            total = values[block] + others[block]
            value = jnp.where(even, total[:28], total[4:])
            out_ref[pl.ds(2 * (first + block) + tile, 28, stride=stride), :] = value * inverse

    def tick(now, _):
        for i in range(ns):
            k = now - by_core(core, [s[i] for s in STARTS])
            length = chain(i)

            if STREAMS[i][0]:

                @pl.when(k == 0)
                def _():
                    if i == second:
                        exchange.wait_recv()

                    @pl.when(core == 0)
                    def _():
                        multiply(i, pair, mine)

                    @pl.when(core == 1)
                    def _():
                        window(i).wait_recv()
                        multiply(i, pair, other)

                    measure(i)

            tick_of(i, k)

            @pl.when(k == length)
            def _():
                finish(i)

            if STREAMS[i][0] == 0:

                @pl.when(k == length + 1)
                def _():
                    deliver(i)

        return 0

    lax.fori_loop(0, TICKS, tick, 0)

    for i in range(second, ns):
        deliver(i)
    exchange.wait_send()

    @pl.when(core == 1)
    def _():
        for i in range(second, ns):
            window(i).wait_send()

    for i in range(ns):
        for d in range(2):

            def sent(k, _):
                message(i, d, k + 1, across).wait_send()
                return 0

            lax.fori_loop(0, depth - (d + i) % 2, sent, 0)
        late(i, 1).wait_send()
        if STREAMS[i][0]:
            late(i, 0).wait_send()


def per_device(acts):
    nz = lax.axis_size("dp") // 2
    depth = nz // 2
    ns = len(STREAMS)
    ring = [p.rows for p in PACKETS]
    swaps = [p.rows for p in SWAPS]
    scratch = [
        pltpu.VMEM((acts.shape[0], COLS), jnp.bfloat16),
        pltpu.VMEM((acts.shape[0], COLS), jnp.bfloat16),
        pltpu.VMEM((acts.shape[0], COLS), jnp.bfloat16),
        pltpu.VMEM((ROWS, COLS), jnp.float32),
        pltpu.VMEM((ROWS, COLS), jnp.float32),
        pltpu.VMEM((ns, nz, 8, LANES), jnp.float32),
    ]
    scratch += [pltpu.VMEM((2, depth + 1, n, LANES), jnp.bfloat16) for n in ring]
    scratch += [pltpu.VMEM((2, depth, n, LANES), jnp.bfloat16) for n in ring]
    scratch += [pltpu.VMEM((2, n, LANES), jnp.bfloat16) for n in swaps] * 2
    scratch += [pltpu.VMEM((32 * BLOCKS, LANES), jnp.float32)]
    dma = pltpu.SemaphoreType.DMA
    scratch += [dma, dma, dma, dma((ns,)), dma((ns,)), dma((ns, 2, depth)), dma((ns, 2, depth)), dma((ns, 2)), dma((ns, 2))]
    half = ROWS // (2 * nz)
    flat = pl.pallas_call(
        lambda *refs: kernel(nz, *refs),
        out_shape=jax.ShapeDtypeStruct((half * 2 * BLOCKS, LANES), jnp.float32),
        in_specs=[pl.BlockSpec(memory_space=pl.ANY)],
        out_specs=pl.BlockSpec(memory_space=pltpu.VMEM),
        scratch_shapes=scratch,
        compiler_params=pltpu.CompilerParams(
            collective_id=0, has_side_effects=True, vmem_limit_bytes=52 * 2**20
        ),
        cost_estimate=pl.CostEstimate(
            flops=4 * ROWS * COLS * acts.shape[0], bytes_accessed=2 * acts.size, transcendentals=0
        ),
    )(acts)
    tiles = flat.reshape(half, BLOCKS, 2, LANES).transpose(0, 2, 1, 3)
    return tiles.reshape(half, 1, 2, COLS)


def solution(mesh):
    return jax.shard_map(
        per_device,
        mesh=mesh,
        in_specs=(P("dp", "tensor"),),
        out_specs=P("dp", "tensor", None, None),
        check_vma=False,
    )
```

time: 352 us -> 68.1 us (0.19)
  blocking collectives: 304 us -> 0 us
  Pallas kernels: 0 us -> 67.1 us
  waiting for transfers between devices: 20.5 us -> 0 us
  local copies, waits for them, and re-layouts: 12.3 us -> 0.82 us
  other arithmetic: 8.42 us -> 0 us
  matrix products: 4.26 us -> 0 us
    all_to_all x1 -> x0, blocking collectives: 304 us -> none  [per_device(): lax.all_to_all(stacked[None], 'dp', split_axis=1, concat_axis=0, tiled=True)]
    pallas_call x0 -> x1, Pallas kernels: none -> 67.1 us  [per_device(): pl.pallas_call(lambda *refs: kernel(nz, *refs), out_shape=jax.ShapeDtypeS...]
    ppermute x1 -> x0, waiting for transfers between devices: 20.5 us -> none  [passed_along(): return lax.ppermute(block, axis, route)]
    broadcast_in_dim x1 -> x0, local copies, waits for them, and re-layouts: 10.5 us -> none  [per_device(): stacked[None]]
    reduce_sum x1 -> x0, other arithmetic: 5.32 us -> none  [per_device(): summed = jnp.sum(shares, axis=0)[:, None, :, :]]
    dot_general x2 -> x0, matrix products: 4.26 us -> none  [tile_rows(): lax.dot_general(window, other, (((0,), (0,)), ((), ())), preferred_elemen...]
  transfers between devices with their start and end apart: 1 -> 0, of which waited for: 1 -> 0; matrix products, arithmetic and copies ran while one was open for 1% -> 0% of each run, Pallas kernels for 0% -> 0%
where the time goes in v2:
time: 68.1 us; the launch traced here: 67.9 us
  Pallas kernels  67.1 us (99%)
  local copies, waits for them, and re-layouts  0.82 us (1%)
    pallas_call x1, Pallas kernels, per_device(): pl.pallas_call(lambda *refs: kernel(nz, *refs), out_shape=jax.ShapeDtypeS...  67.1 us

profile of v2, /device:TPU:24, one launch (start us, length us, event | category | flops | bytes accessed | tf_op | source)
XLA Modules:
  0.0 67.9 jit_solution(15210548119980355254)
XLA Ops:
  0.0 67.1 %shard_map.17 = f32[392,128]{1,0:T(8,128)S(1)} custom-call(bf16[1024,1792]{1,0:T(8,128)(2,1)} %refs_0_.1), custom_call_target="tpu_custom_call" | custom-call | flops 3288334336 | bytes 3670016 | tf_op jit(solution)/shard_map/pallas_call | solution.py:384
  67.1 0.8 %reshape.7 = f32[28,1,2,896]{3,2,0,1:T(2,128)} reshape(f32[28,2,7,128]{3,2,1,0:T(8,128)S(1)} %bitcast.6) | data formatting | bytes 401408 | tf_op jit(solution)/shard_map/reshape | solution.py:398
  (1 shorter events, 0.0 us)

commit v3 on v2

--- a/solution.py
+++ b/solution.py
@@ -15,7 +15,7 @@
 POWER = 17
 TOP = 2.0**7.375
 
-STREAMS = ((0, 0, 4), (0, 4, 3), (1, 0, 4), (1, 4, 3))
+STREAMS = ((0, 0, 4), (0, 4, 3), (1, 0, 3), (1, 3, 4))
 STARTS = ((0, 0, 0, 0), (0, 0, 2, 5))
 CHAINS = ((8, 8, 8, 8), (8, 8, 8, 4))
 PIECES = 2
@@ -91,7 +91,7 @@
 SWAPS = tuple(Packet((32,) * n) for _, _, n in STREAMS)
 
 
-def kernel(nz, acts_ref, out_ref, mine, pair, other, part0, part1, peaks, *rest):
+def kernel(nz, acts_ref, out_ref, mine, pair, other, part0, part1, *rest):
     ns = len(STREAMS)
     got, put, late_got, late_put = (rest[k * ns : (k + 1) * ns] for k in range(4))
     kept, load_sem, psend, precv, wsend, wrecv, rsend, rrecv, lsend, lrecv = rest[4 * ns :]
@@ -151,16 +151,6 @@
             left_ref[...], right_ref[:, a:b], TN, preferred_element_type=jnp.float32
         )
 
-    def measure(i):
-        def peak(owner, _):
-            peaks[i, owner] = tops(own_rows(i, owner))
-            return 0
-
-        lax.fori_loop(0, nz, peak, 0)
-
-    for i in range(second):
-        multiply(i, mine, mine)
-        measure(i)
     pl.semaphore_wait(barrier, len(partners))
 
     exchange = pltpu.make_async_remote_copy(
@@ -189,6 +179,9 @@
         for i in range(second, ns):
             window(i).start()
 
+    for i in range(second):
+        multiply(i, mine, mine)
+
     def reach(i, d):
         return depth - lax.rem(d + i, 2)
 
@@ -225,7 +218,8 @@
         def _():
             message(i, d, hop + 1, across).wait_recv()
 
-        values, bound = own_rows(i, owner), peaks[i, owner]
+        values = own_rows(i, owner)
+        bound = tops(values)
         more, more_bound = PACKETS[i].read(got[i].at[d, jnp.where(outermost, depth, hop)])
         PACKETS[i].write(add(values, more), put[i].at[d, hop - 1], bound + more_bound)
         jump = jnp.where(lax.rem(hop, length) == 1, hop, 1)
@@ -248,7 +242,8 @@
 
     def gather(i):
         length = chain(i)
-        values, bound = own_rows(i, z), peaks[i, z]
+        values = own_rows(i, z)
+        bound = tops(values)
         for m in range(PIECES):
             for d in range(2):
                 hop = m * length + 1
@@ -263,7 +258,6 @@
         return values, bound
 
     inverse = 1.0 / (1024 * ndp)
-    stride = 2 * BLOCKS
 
     def finish(i):
         tile, _, blocks = STREAMS[i]
@@ -297,7 +291,8 @@
         for block in range(blocks):
             total = values[block] + others[block]
             value = jnp.where(even, total[:28], total[4:])
-            out_ref[pl.ds(2 * (first + block) + tile, 28, stride=stride), :] = value * inverse
+            at = (first + block) * LANES
+            out_ref[:, tile, at : at + LANES] = value * inverse
 
     def tick(now, _):
         for i in range(ns):
@@ -320,7 +315,6 @@
                         window(i).wait_recv()
                         multiply(i, pair, other)
 
-                    measure(i)
 
             tick_of(i, k)
 
@@ -372,7 +366,6 @@
         pltpu.VMEM((acts.shape[0], COLS), jnp.bfloat16),
         pltpu.VMEM((ROWS, COLS), jnp.float32),
         pltpu.VMEM((ROWS, COLS), jnp.float32),
-        pltpu.VMEM((ns, nz, 8, LANES), jnp.float32),
     ]
     scratch += [pltpu.VMEM((2, depth + 1, n, LANES), jnp.bfloat16) for n in ring]
     scratch += [pltpu.VMEM((2, depth, n, LANES), jnp.bfloat16) for n in ring]
@@ -381,9 +374,9 @@
     dma = pltpu.SemaphoreType.DMA
     scratch += [dma, dma, dma, dma((ns,)), dma((ns,)), dma((ns, 2, depth)), dma((ns, 2, depth)), dma((ns, 2)), dma((ns, 2))]
     half = ROWS // (2 * nz)
-    flat = pl.pallas_call(
+    tiles = pl.pallas_call(
         lambda *refs: kernel(nz, *refs),
-        out_shape=jax.ShapeDtypeStruct((half * 2 * BLOCKS, LANES), jnp.float32),
+        out_shape=jax.ShapeDtypeStruct((half, 2, COLS), jnp.float32),
         in_specs=[pl.BlockSpec(memory_space=pl.ANY)],
         out_specs=pl.BlockSpec(memory_space=pltpu.VMEM),
         scratch_shapes=scratch,
@@ -394,7 +387,6 @@
             flops=4 * ROWS * COLS * acts.shape[0], bytes_accessed=2 * acts.size, transcendentals=0
         ),
     )(acts)
-    tiles = flat.reshape(half, BLOCKS, 2, LANES).transpose(0, 2, 1, 3)
     return tiles.reshape(half, 1, 2, COLS)
 
 

time: 68.1 us -> 66 us (0.969)
  the two profiles are of different devices: /device:TPU:24 before, /device:TPU:64 now
where the time goes in v3:
time: 66 us; the launch traced here: 65.9 us
  Pallas kernels  65.2 us (99%)
  local copies, waits for them, and re-layouts  0.68 us (1%)
    pallas_call x1, Pallas kernels, per_device(): pl.pallas_call(lambda *refs: kernel(nz, *refs), out_shape=jax.ShapeDtypeS...  65.2 us

profile of v3, /device:TPU:64, one launch (start us, length us, event | category | flops | bytes accessed | tf_op | source)
XLA Modules:
  0.0 65.9 jit_solution(9888817819320020336)
XLA Ops:
  0.0 65.2 %shard_map.17 = f32[28,2,896]{2,1,0:T(2,128)S(1)} custom-call(bf16[1024,1792]{1,0:T(8,128)(2,1)} %refs_0_.1), custom_call_target="tpu_custom_call" | custom-call | flops 3288334336 | bytes 3670016 | tf_op jit(solution)/shard_map/pallas_call | solution.py:377
  65.2 0.7 %copy.4 = f32[28,1,2,896]{3,2,1,0:T(2,128)} copy(f32[28,1,2,896]{3,2,1,0:T(2,128)S(1)} %bitcast.3) | data formatting | bytes 401408

commit v4 on v3

--- a/solution.py
+++ b/solution.py
@@ -179,8 +179,7 @@
         for i in range(second, ns):
             window(i).start()
 
-    for i in range(second):
-        multiply(i, mine, mine)
+    part0[...] = lax.dot_general(mine[...], mine[...], TN, preferred_element_type=jnp.float32)
 
     def reach(i, d):
         return depth - lax.rem(d + i, 2)

time: 66 us -> 66 us (level)
  no operation moved by 1% of the time
where the time goes in v4:
time: 66 us; the launch traced here: 65.9 us
  Pallas kernels  65.2 us (99%)
  local copies, waits for them, and re-layouts  0.68 us (1%)
    pallas_call x1, Pallas kernels, per_device(): pl.pallas_call(lambda *refs: kernel(nz, *refs), out_shape=jax.ShapeDtypeS...  65.2 us

profile of v4, /device:TPU:64, one launch (start us, length us, event | category | flops | bytes accessed | tf_op | source)
XLA Modules:
  0.0 65.9 jit_solution(2972186804115794554)
XLA Ops:
  0.0 65.2 %shard_map.17 = f32[28,2,896]{2,1,0:T(2,128)S(1)} custom-call(bf16[1024,1792]{1,0:T(8,128)(2,1)} %refs_0_.1), custom_call_target="tpu_custom_call" | custom-call | flops 3288334336 | bytes 3670016 | tf_op jit(solution)/shard_map/pallas_call | solution.py:376
  65.2 0.7 %copy.4 = f32[28,1,2,896]{3,2,1,0:T(2,128)} copy(f32[28,1,2,896]{3,2,1,0:T(2,128)S(1)} %bitcast.3) | data formatting | bytes 401408

commit v5 on v3

--- a/solution.py
+++ b/solution.py
@@ -16,7 +16,7 @@
 TOP = 2.0**7.375
 
 STREAMS = ((0, 0, 4), (0, 4, 3), (1, 0, 3), (1, 3, 4))
-STARTS = ((0, 0, 0, 0), (0, 0, 2, 5))
+STARTS = ((0, 0, 0, 1), (0, 0, 2, 5))
 CHAINS = ((8, 8, 8, 8), (8, 8, 8, 4))
 PIECES = 2
 JUMPS = (1, 5)

time: 66 us -> 66.5 us (level)
  the two profiles are of different devices: /device:TPU:64 before, /device:TPU:24 now
where the time goes in v5:
time: 66.5 us; the launch traced here: 65.2 us
  Pallas kernels  64.5 us (97%)
  local copies, waits for them, and re-layouts  0.68 us (1%)
    pallas_call x1, Pallas kernels, per_device(): pl.pallas_call(lambda *refs: kernel(nz, *refs), out_shape=jax.ShapeDtypeS...  64.5 us

profile of v5, /device:TPU:24, one launch (start us, length us, event | category | flops | bytes accessed | tf_op | source)
XLA Modules:
  0.0 65.2 jit_solution(7999385589171925593)
XLA Ops:
  0.0 64.5 %shard_map.17 = f32[28,2,896]{2,1,0:T(2,128)S(1)} custom-call(bf16[1024,1792]{1,0:T(8,128)(2,1)} %refs_0_.1), custom_call_target="tpu_custom_call" | custom-call | flops 3288334336 | bytes 3670016 | tf_op jit(solution)/shard_map/pallas_call | solution.py:377
  64.5 0.7 %copy.4 = f32[28,1,2,896]{3,2,1,0:T(2,128)} copy(f32[28,1,2,896]{3,2,1,0:T(2,128)S(1)} %bitcast.3) | data formatting | bytes 401408
